TPU v7x, 512 devices: a whole 4x4x16 slice. The times are simulated.
512 devices in a mesh: ctx: 32 (over y, x, core), tp: 16 (over z).
Axes of the slice: x: 4, y: 4, z: 16, core: 2. Of those that a mesh axis runs over, the one named last changes fastest.
Arguments:
- features: bfloat16 [8192, 3, 4096], P('ctx', None, 'tp'), may hold values from -6 to 6
- short_taps: float32 [3, 3, 4096], P(None, None, 'tp'), may hold values from -3.5 to 3.5
- residues: float32 [16, 256], P(None, 'tp'), may hold values from -1.5 to 1.5
- rates: float32 [16, 256], P(None, 'tp'), may hold values from 3.6621094e-05 to 0.05, as said below
- skip: float32 [4096], P('tp'), may hold values from -4 to 4
- out_weight: bfloat16 [4096, 4096], P(None, 'tp'), may hold values from -0.09375 to 0.09375
Outputs:
- mixed: bfloat16 [8192, 4096], P('ctx', 'tp')
Inputs may be any that keep to these rules, and one draw needn't show every extreme that they name: `rates`: decay rate of one mode of one filter.
All inputs are finite; a program needn't handle non-finite values.
Results may differ from a plain program's by a relative error of at most 0.0049.
Values may be sent and summed in bfloat16 or wider, within the bound.
No kernel may reach another device: no remote copies, remote signals or barrier semaphores. Data moves between devices by JAX's collectives and lax.ppermute only.
A program may use at most 128 MiB of HBM per device.

v0:
```python
import math
import jax
import jax.numpy as jnp
from jax import lax
from jax.sharding import PartitionSpec as P

SHORT = 3


def passed_along(array, axis, by):
    count = lax.axis_size(axis)
    pairs = [(i, i + by) for i in range(count) if 0 <= i + by < count]
    return lax.ppermute(array, axis, pairs)


def regroup(block):
    return lax.all_to_all(block, "ctx", split_axis=0, concat_axis=0, tiled=True)


def mixdot(form, left, right):
    return jnp.einsum(form, left, right, precision=lax.Precision.HIGHEST)


def rotate(real_part, imag_part, cosine, sine, sign):
    return (
        real_part * cosine - sign * imag_part * sine,
        imag_part * cosine + sign * real_part * sine,
    )


def phase_table(numer, denom):
    angle = 2.0 * math.pi / denom * numer.astype(jnp.float32)
    return (jnp.cos(angle), jnp.sin(angle))


def filter_spectrum(residues, rates, own, rows, ctx_count):
    twice = 2 * ctx_count
    seq_len = rows * ctx_count
    total_len = 2 * seq_len
    sub_index = jnp.arange(2, dtype=jnp.int32)[:, None]
    freq_index = jnp.arange(rows, dtype=jnp.int32)[None, :]
    wave = 2 * own + sub_index + twice * freq_index
    signed = jnp.where(wave < seq_len, wave, wave - total_len)
    theta = 2.0 * math.pi / total_len * signed.astype(jnp.float32)
    theta = theta[None, :, :, None]
    decay = rates[:, None, None, :]
    damping = jnp.exp(-decay)
    den_real = -jnp.expm1(-decay) + damping * 2.0 * jnp.sin(0.5 * theta) ** 2
    den_imag = damping * jnp.sin(theta)
    parity = (1 - 2 * sub_index).astype(jnp.float32)[None, :, :, None]
    numer = 1.0 - jnp.exp(-decay * float(seq_len)) * parity
    scaled = (
        residues[:, None, None, :]
        * jnp.sqrt(2.0 * decay)
        * numer
        / (den_real * den_real + den_imag * den_imag)
    )
    return (jnp.sum(scaled * den_real, axis=0), -jnp.sum(scaled * den_imag, axis=0))


def transform_conv(product, residues, rates, ctx_count, own):
    rows = product.shape[0]
    width = product.shape[1]
    filters = residues.shape[1]
    piece = rows // ctx_count
    twice = 2 * ctx_count
    total_len = 2 * rows * ctx_count
    dev_index = jnp.arange(ctx_count, dtype=jnp.int32)
    freq_group = jnp.arange(twice, dtype=jnp.int32)
    cos_outer, sin_outer = phase_table(freq_group[:, None] * dev_index[None, :] % twice, twice)
    local_pos = own * piece + jnp.arange(piece, dtype=jnp.int32)
    cos_twist, sin_twist = phase_table(
        freq_group[:, None] * local_pos[None, :] % total_len, total_len
    )
    cos_twist = cos_twist[:, :, None]
    sin_twist = sin_twist[:, :, None]
    row_index = jnp.arange(rows, dtype=jnp.int32)
    cos_inner, sin_inner = phase_table(row_index[:, None] * row_index[None, :] % rows, rows)
    cos_inner = cos_inner.reshape(rows, ctx_count, piece)
    sin_inner = sin_inner.reshape(rows, ctx_count, piece)
    moved = regroup(product.reshape(ctx_count, piece, width))
    spec_real = mixdot("ca,ajm->cjm", cos_outer, moved)
    spec_imag = -mixdot("ca,ajm->cjm", sin_outer, moved)
    spec_real, spec_imag = rotate(spec_real, spec_imag, cos_twist, sin_twist, -1.0)
    outgoing = jnp.concatenate([spec_real, spec_imag], -1).reshape(ctx_count, 2 * piece, 2 * width)
    arrived = regroup(outgoing).reshape(ctx_count, 2, piece, 2 * width)
    arr_real = arrived[..., :width]
    arr_imag = arrived[..., width:]
    freq_real = mixdot("usj,scjm->cum", cos_inner, arr_real) + mixdot(
        "usj,scjm->cum", sin_inner, arr_imag
    )
    freq_imag = mixdot("usj,scjm->cum", cos_inner, arr_imag) - mixdot(
        "usj,scjm->cum", sin_inner, arr_real
    )
    filt_real, filt_imag = filter_spectrum(residues, rates, own, rows, ctx_count)
    filt_real = filt_real[..., None]
    filt_imag = filt_imag[..., None]
    freq_real = freq_real.reshape(2, rows, filters, width // filters)
    freq_imag = freq_imag.reshape(2, rows, filters, width // filters)
    prod_real = (freq_real * filt_real - freq_imag * filt_imag).reshape(2, rows, width)
    prod_imag = (freq_real * filt_imag + freq_imag * filt_real).reshape(2, rows, width)
    back_real = mixdot("usj,cum->scjm", cos_inner, prod_real) - mixdot(
        "usj,cum->scjm", sin_inner, prod_imag
    )
    back_imag = mixdot("usj,cum->scjm", sin_inner, prod_real) + mixdot(
        "usj,cum->scjm", cos_inner, prod_imag
    )
    returning = jnp.concatenate([back_real, back_imag], -1).reshape(ctx_count, 2 * piece, 2 * width)
    returned = regroup(returning).reshape(twice, piece, 2 * width)
    ret_real, ret_imag = rotate(
        returned[..., :width], returned[..., width:], cos_twist, sin_twist, 1.0
    )
    scale = 1.0 / total_len
    out_real = mixdot("ca,cjm->ajm", cos_outer, ret_real) - mixdot(
        "ca,cjm->ajm", sin_outer, ret_imag
    )
    time_rows = out_real * scale
    conv = regroup(time_rows).reshape(rows, width)
    return conv


def shards(features, short_taps, residues, rates, skip, out_weight):
    ctx_count = lax.axis_size("ctx")
    own = lax.axis_index("ctx")
    rows = features.shape[0]
    rim = passed_along(features[rows - (SHORT - 1) :], "ctx", 1)
    extended = jnp.concatenate([rim, features], 0)
    shorted = jnp.zeros(features.shape, jnp.float32)
    for shift in range(SHORT):
        window = extended[SHORT - 1 - shift : SHORT - 1 - shift + rows].astype(jnp.float32)
        shorted = shorted + short_taps[shift] * window
    query = shorted[:, 0, :]
    product = shorted[:, 1, :] * shorted[:, 2, :]
    conv = transform_conv(product, residues, rates, ctx_count, own)
    gated = (query * (conv + skip * product)).astype(jnp.bfloat16)
    projected = jnp.dot(
        lax.all_gather(gated, "tp", axis=1, tiled=True),
        out_weight,
        preferred_element_type=jnp.float32,
    )
    return projected.astype(jnp.bfloat16)


def solution(mesh):
    in_specs = (
        P("ctx", None, "tp"),
        P(None, None, "tp"),
        P(None, "tp"),
        P(None, "tp"),
        P("tp"),
        P(None, "tp"),
    )
    out_specs = P("ctx", "tp")
    return jax.shard_map(shards, mesh=mesh, in_specs=in_specs, out_specs=out_specs, check_vma=False)
```

profile of v0, /device:TPU:32, one launch (start us, length us, event | category | flops | bytes accessed | tf_op | source)
XLA Modules:
  0.0 198.4 jit_solution(7042605041022296858)
XLA Ops:
  6.5 0.9 slice.41
  7.4 1.7 collective-permute-start
  9.9 1.8 multiply_add_fusion
  12.5 9.7 %all-to-all-start = ((f32[32,8,256]{2,1,0:T(8,128)}), f32[32,8,256]{2,1,0:T(8,128)S(1)}, u32[]{:S(2)}, u32[]{:S(2)}) async-start(f32[32,8,256]{2,1,0:T(8,128)} %fusion.68), calls=%async_computation | async-start | bytes 524288 | tf_op jit(solution)/shard_map/all_to_all | solution.py:17
  22.3 8.8 %all-to-all-done = f32[32,8,256]{2,1,0:T(8,128)S(1)} async-done(((f32[32,8,256]{2,1,0:T(8,128)}), f32[32,8,256]{2,1,0:T(8,128)S(1)}, u32[]{:S(2)}, u32[]{:S(2)}) %all-to-all-start) | async-done | bytes 262176 | tf_op jit(solution)/shard_map/all_to_all | solution.py:17
  31.8 0.8 multiply_subtract_fusion
  32.8 1.6 copy.36
  34.4 4.7 %all-to-all-start.1 = ((f32[32,16,512]{2,1,0:T(8,128)}), f32[32,16,512]{2,1,0:T(8,128)}, u32[]{:S(2)}, u32[]{:S(2)}) async-start(f32[32,16,512]{2,1,0:T(8,128)} %bitcast.118), calls=%async_computation.1 | async-start | bytes 2097152 | tf_op jit(solution)/shard_map/all_to_all | solution.py:17
  39.9 16.5 %all-to-all-done.1 = f32[32,16,512]{2,1,0:T(8,128)} async-done(((f32[32,16,512]{2,1,0:T(8,128)}), f32[32,16,512]{2,1,0:T(8,128)}, u32[]{:S(2)}, u32[]{:S(2)}) %all-to-all-start.1) | async-done | bytes 1048608 | tf_op jit(solution)/shard_map/all_to_all | solution.py:17
  56.4 1.8 copy.37
  58.2 1.9 convolution_bitcast_fusion.2
  60.1 1.9 convolution_bitcast_fusion
  62.0 1.9 fusion.3
  63.9 1.9 fusion.11
  65.9 1.6 fusion.14
  67.5 1.8 fusion.16
  69.3 1.6 fusion
  70.9 1.6 fusion.1
  73.2 20.6 %all_to_all.20 = f32[32,16,512]{2,1,0:T(8,128)S(1)} all-to-all(f32[32,16,512]{2,1,0:T(8,128)S(1)} %copy.42), channel_id=1, replica_groups=mesh['ctx'=32,'tp'=16] {'ctx'}, dimensions={0} | all-to-all | bytes 2097152 | tf_op jit(solution)/shard_map/all_to_all | solution.py:17
  94.0 0.8 fusion.21
  94.7 0.8 fusion.6
  95.7 12.3 %all_to_all.21 = f32[32,8,256]{2,1,0:T(8,128)S(1)} all-to-all(f32[32,8,256]{2,1,0:T(8,128)S(1)} %copy.45), channel_id=1, replica_groups=mesh['ctx'=32,'tp'=16] {'ctx'}, dimensions={0} | all-to-all | bytes 524288 | tf_op jit(solution)/shard_map/all_to_all | solution.py:17
  108.7 79.9 %all-gather.2.cloned.1.call-done = bf16[256,4096]{1,0:T(8,128)(2,1)} async-done(((bf16[256,256]{1,0:T(8,128)(2,1)}), bf16[256,4096]{1,0:T(8,128)(2,1)}) %all-gather.2.cloned.1.call-update) | async-done | bytes 2097168 | tf_op jit(solution)/shard_map/all_gather | solution.py:137
  188.6 3.0 %convolution_convert_fusion = bf16[256,256]{1,0:T(8,128)(2,1)} fusion(bf16[256,4096]{1,0:T(8,128)(2,1)} %all-gather.2.cloned.1.call-done, bf16[4096,256]{1,0:T(8,128)(2,1)S(1)} %copy-done), kind=kOutput, calls=%fused_computation.15 | convolution fusion | flops 536936448 | bytes 4325376 | tf_op jit(solution)/shard_map/dot_general | solution.py:136
  (31 shorter events, 5.0 us)
Async XLA Ops:
  6.5 182.0 %copy-start = (bf16[4096,256]{1,0:T(8,128)(2,1)S(1)}, bf16[4096,256]{1,0:T(8,128)(2,1)}, u32[]{:S(2)}) copy-start(bf16[4096,256]{1,0:T(8,128)(2,1)} %param.11) | copy-start | bytes 6291460
  7.4 2.5 %collective-permute-start = (bf16[2,3,256]{2,0,1:T(2,128)(2,1)S(1)}, bf16[2,3,256]{2,0,1:T(2,128)(2,1)S(1)}, u32[]{:S(2)}, u32[]{:S(2)}) collective-permute-start(bf16[2,3,256]{2,0,1:T(2,128)(2,1)S(1)} %slice.41), channel_id=1, source_target_pairs={{0,16},{16,32},{32,48},{48,64},{64,80},{80,96},{96,112},{112,128},... | collective-permute-start | bytes 9224 | tf_op jit(solution)/shard_map/ppermute | solution.py:13
  12.5 18.6 %all-to-all-start = ((f32[32,8,256]{2,1,0:T(8,128)}), f32[32,8,256]{2,1,0:T(8,128)S(1)}, u32[]{:S(2)}, u32[]{:S(2)}) async-start(f32[32,8,256]{2,1,0:T(8,128)} %fusion.68), calls=%async_computation | async-start | bytes 524288 | tf_op jit(solution)/shard_map/all_to_all | solution.py:17
  32.8 6.7 %copy-start.1 = (f32[16,16]{1,0:T(8,128)S(1)}, f32[16,16]{1,0:T(8,128)}, u32[]{:S(2)}) copy-start(f32[16,16]{1,0:T(8,128)} %param.8) | copy-start | bytes 3076
  32.8 6.7 %copy-start.2 = (f32[16,16]{1,0:T(8,128)S(1)}, f32[16,16]{1,0:T(8,128)}, u32[]{:S(2)}) copy-start(f32[16,16]{1,0:T(8,128)} %param.9) | copy-start | bytes 3076
  34.4 22.0 %all-to-all-start.1 = ((f32[32,16,512]{2,1,0:T(8,128)}), f32[32,16,512]{2,1,0:T(8,128)}, u32[]{:S(2)}, u32[]{:S(2)}) async-start(f32[32,16,512]{2,1,0:T(8,128)} %bitcast.118), calls=%async_computation.1 | async-start | bytes 2097152 | tf_op jit(solution)/shard_map/all_to_all | solution.py:17
  39.1 149.5 %all-gather.2.cloned.1.call-start = ((), (), s32[]{:S(2)}) async-start(), calls=%async_computation.4 | async-start | bytes 2228224 | tf_op jit(solution)/shard_map/all_gather | solution.py:137
  94.0 14.0 %copy-start.3 = (f32[256]{0:T(256)S(1)}, f32[256]{0:T(256)}, u32[]{:S(2)}) copy-start(f32[256]{0:T(256)} %param.10) | copy-start | bytes 3076
Sparse Core Ops, SparseCore 0:
  108.8 79.7 all-gather.1
where the time goes:
time: 199 us; the launch traced here: 198 us
  waiting for transfers between devices  105 us (53%)
  blocking collectives  32.9 us (17%)
  matrix products  20.2 us (10%)
  starting transfers between devices  16.3 us (8%)
  between operations  13.7 us (7%)
  local copies, waits for them, and re-layouts  5.9 us (3%)
  other arithmetic  4.2 us (2%)
    all_gather x1, waiting for transfers between devices, shards(): lax.all_gather(gated, 'tp', axis=1, tiled=True)  79.9 us
    all_to_all x2, blocking collectives, regroup(): return lax.all_to_all(block, 'ctx', split_axis=0, concat_axis=0, tiled=True)  32.9 us
    all_to_all x2, waiting for transfers between devices, regroup(): return lax.all_to_all(block, 'ctx', split_axis=0, concat_axis=0, tiled=True)  25.2 us
    dot_general x12, matrix products, mixdot(): return jnp.einsum(form, left, right, precision=lax.Precision.HIGHEST)  17.2 us
    all_to_all x2, starting transfers between devices, regroup(): return lax.all_to_all(block, 'ctx', split_axis=0, concat_axis=0, tiled=True)  14.4 us
  transfers between devices with their start and end apart: 4, of which 4 were waited for; matrix products, arithmetic and copies ran while one was open for 1% of the time, Pallas kernels for 0%

commit v1 on v0

--- a/solution.py
+++ b/solution.py
@@ -133,11 +133,19 @@
     product = shorted[:, 1, :] * shorted[:, 2, :]
     conv = transform_conv(product, residues, rates, ctx_count, own)
     gated = (query * (conv + skip * product)).astype(jnp.bfloat16)
-    projected = jnp.dot(
-        lax.all_gather(gated, "tp", axis=1, tiled=True),
-        out_weight,
-        preferred_element_type=jnp.float32,
-    )
+
+    def put_lines(message):
+        return jnp.concatenate(
+            lax.all_to_all(
+                jnp.stack(lax.axis_size("tp") * [message]),
+                axis_name="tp",
+                split_axis=0,
+                concat_axis=0,
+            ),
+            1,
+        )
+
+    projected = jnp.dot(put_lines(gated), out_weight, preferred_element_type=jnp.float32)
     return projected.astype(jnp.bfloat16)
 
 

time: 199 us -> 216 us (1.085)
  blocking collectives: 32.9 us -> 145 us
  waiting for transfers between devices: 105 us -> 25.4 us
  between operations: 13.7 us -> 0.28 us
    all_to_all x0 -> x1, blocking collectives: none -> 112 us  [put_lines(): lax.all_to_all(jnp.stack(lax.axis_size('tp') * [message]), axis_name='tp'...]
    all_gather x1 -> x0, waiting for transfers between devices: 79.9 us -> none  [shards(): lax.all_gather(gated, 'tp', axis=1, tiled=True)]
  transfers between devices with their start and end apart: 4 -> 3, of which waited for: 4 -> 3; matrix products, arithmetic and copies ran while one was open for 1% -> 1% of each run, Pallas kernels for 0% -> 0%
where the time goes in v1:
time: 216 us; the launch traced here: 215 us
  blocking collectives  145 us (67%)
  waiting for transfers between devices  25.4 us (12%)
  matrix products  18.6 us (9%)
  starting transfers between devices  16.3 us (8%)
  local copies, waits for them, and re-layouts  6.2 us (3%)
  other arithmetic  3.53 us (2%)
    all_to_all x1, blocking collectives, put_lines(): lax.all_to_all(jnp.stack(lax.axis_size('tp') * [message]), axis_name='tp'...  112 us
    all_to_all x2, blocking collectives, regroup(): return lax.all_to_all(block, 'ctx', split_axis=0, concat_axis=0, tiled=True)  32.9 us
    all_to_all x2, waiting for transfers between devices, regroup(): return lax.all_to_all(block, 'ctx', split_axis=0, concat_axis=0, tiled=True)  25.3 us
    dot_general x12, matrix products, mixdot(): return jnp.einsum(form, left, right, precision=lax.Precision.HIGHEST)  17.2 us
    all_to_all x2, starting transfers between devices, regroup(): return lax.all_to_all(block, 'ctx', split_axis=0, concat_axis=0, tiled=True)  14.5 us
  transfers between devices with their start and end apart: 3, of which 3 were waited for; matrix products, arithmetic and copies ran while one was open for 1% of the time, Pallas kernels for 0%

profile of v1, /device:TPU:32, one launch (start us, length us, event | category | flops | bytes accessed | tf_op | source)
XLA Modules:
  0.0 215.3 jit_solution(5684108391675253431)
XLA Ops:
  0.0 0.9 slice.41
  0.9 1.7 collective-permute-start
  3.4 1.8 multiply_add_fusion
  6.0 9.7 %all-to-all-start = ((f32[32,8,256]{2,1,0:T(8,128)}), f32[32,8,256]{2,1,0:T(8,128)S(1)}, u32[]{:S(2)}, u32[]{:S(2)}) async-start(f32[32,8,256]{2,1,0:T(8,128)} %fusion.68), calls=%async_computation | async-start | bytes 524288 | tf_op jit(solution)/shard_map/all_to_all | solution.py:17
  15.8 8.8 %all-to-all-done = f32[32,8,256]{2,1,0:T(8,128)S(1)} async-done(((f32[32,8,256]{2,1,0:T(8,128)}), f32[32,8,256]{2,1,0:T(8,128)S(1)}, u32[]{:S(2)}, u32[]{:S(2)}) %all-to-all-start) | async-done | bytes 262176 | tf_op jit(solution)/shard_map/all_to_all | solution.py:17
  25.3 0.8 multiply_subtract_fusion
  26.2 1.6 copy.38
  27.9 4.8 %all-to-all-start.1 = ((f32[32,16,512]{2,1,0:T(8,128)}), f32[32,16,512]{2,1,0:T(8,128)}, u32[]{:S(2)}, u32[]{:S(2)}) async-start(f32[32,16,512]{2,1,0:T(8,128)} %bitcast.121), calls=%async_computation.1 | async-start | bytes 2097152 | tf_op jit(solution)/shard_map/all_to_all | solution.py:17
  33.3 16.5 %all-to-all-done.1 = f32[32,16,512]{2,1,0:T(8,128)} async-done(((f32[32,16,512]{2,1,0:T(8,128)}), f32[32,16,512]{2,1,0:T(8,128)}, u32[]{:S(2)}, u32[]{:S(2)}) %all-to-all-start.1) | async-done | bytes 1048608 | tf_op jit(solution)/shard_map/all_to_all | solution.py:17
  49.8 1.8 copy.39
  51.7 1.9 convolution_bitcast_fusion
  53.6 1.9 convolution_bitcast_fusion.2
  55.5 1.9 fusion.3
  57.4 1.9 fusion.11
  59.3 1.6 fusion.14
  60.9 1.8 fusion.16
  62.7 1.6 fusion.1
  64.3 1.6 fusion
  66.7 20.6 %all_to_all.25 = f32[32,16,512]{2,1,0:T(8,128)S(1)} all-to-all(f32[32,16,512]{2,1,0:T(8,128)S(1)} %copy.44), channel_id=1, replica_groups=mesh['ctx'=32,'tp'=16] {'ctx'}, dimensions={0} | all-to-all | bytes 2097152 | tf_op jit(solution)/shard_map/all_to_all | solution.py:17
  87.4 0.7 fusion.21
  88.2 0.8 fusion.6
  89.1 12.3 %all_to_all.26 = f32[32,8,256]{2,1,0:T(8,128)S(1)} all-to-all(f32[32,8,256]{2,1,0:T(8,128)S(1)} %copy.47), channel_id=1, replica_groups=mesh['ctx'=32,'tp'=16] {'ctx'}, dimensions={0} | all-to-all | bytes 524288 | tf_op jit(solution)/shard_map/all_to_all | solution.py:17
  101.8 112.1 %all_to_all.27 = bf16[16,256,256]{1,2,0:T(8,128)(2,1)S(1)} all-to-all(bf16[16,256,256]{1,2,0:T(8,128)(2,1)S(1)} %stack.2), channel_id=1, replica_groups=mesh['ctx'=32,'tp'=16] {'tp'}, dimensions={0} | all-to-all | bytes 4194304 | tf_op jit(solution)/shard_map/all_to_all | solution.py:139
  213.9 1.4 convolution_convert_fusion
  (31 shorter events, 4.4 us)
Async XLA Ops:
  0.0 213.9 %copy-start = (bf16[4096,256]{1,0:T(8,128)(2,1)S(1)}, bf16[4096,256]{1,0:T(8,128)(2,1)}, u32[]{:S(2)}) copy-start(bf16[4096,256]{1,0:T(8,128)(2,1)} %param.11) | copy-start | bytes 6291460
  0.9 2.5 %collective-permute-start = (bf16[2,3,256]{2,0,1:T(2,128)(2,1)S(1)}, bf16[2,3,256]{2,0,1:T(2,128)(2,1)S(1)}, u32[]{:S(2)}, u32[]{:S(2)}) collective-permute-start(bf16[2,3,256]{2,0,1:T(2,128)(2,1)S(1)} %slice.41), channel_id=1, source_target_pairs={{0,16},{16,32},{32,48},{48,64},{64,80},{80,96},{96,112},{112,128},... | collective-permute-start | bytes 9224 | tf_op jit(solution)/shard_map/ppermute | solution.py:13
  6.0 18.6 %all-to-all-start = ((f32[32,8,256]{2,1,0:T(8,128)}), f32[32,8,256]{2,1,0:T(8,128)S(1)}, u32[]{:S(2)}, u32[]{:S(2)}) async-start(f32[32,8,256]{2,1,0:T(8,128)} %fusion.68), calls=%async_computation | async-start | bytes 524288 | tf_op jit(solution)/shard_map/all_to_all | solution.py:17
  26.2 6.6 %copy-start.1 = (f32[16,16]{1,0:T(8,128)S(1)}, f32[16,16]{1,0:T(8,128)}, u32[]{:S(2)}) copy-start(f32[16,16]{1,0:T(8,128)} %param.8) | copy-start | bytes 3076
  26.2 6.6 %copy-start.2 = (f32[16,16]{1,0:T(8,128)S(1)}, f32[16,16]{1,0:T(8,128)}, u32[]{:S(2)}) copy-start(f32[16,16]{1,0:T(8,128)} %param.9) | copy-start | bytes 3076
  27.9 22.0 %all-to-all-start.1 = ((f32[32,16,512]{2,1,0:T(8,128)}), f32[32,16,512]{2,1,0:T(8,128)}, u32[]{:S(2)}, u32[]{:S(2)}) async-start(f32[32,16,512]{2,1,0:T(8,128)} %bitcast.121), calls=%async_computation.1 | async-start | bytes 2097152 | tf_op jit(solution)/shard_map/all_to_all | solution.py:17
  87.4 14.0 %copy-start.3 = (f32[256]{0:T(256)S(1)}, f32[256]{0:T(256)}, u32[]{:S(2)}) copy-start(f32[256]{0:T(256)} %param.10) | copy-start | bytes 3076
